TPU v7x, 32 devices: a whole 2x2x4 slice. The times are simulated.
32 devices in a mesh: seq: 4 (over y, x), dp: 8 (over z, core).
Axes of the slice: x: 2, y: 2, z: 4, core: 2. Of those that a mesh axis runs over, the one named last changes fastest.
Arguments:
- attn_out: bfloat16 [16384, 3072], P('dp', 'seq'), may hold values from -6 to 6
- cotangent: bfloat16 [16384, 3072], P(('seq', 'dp')), may hold values from -0.09375 to 0.09375
- gate: float32 [8, 3072], P('dp'), may hold values from -4 to 4
- weight: float32 [3072, 3072], P('dp', 'seq'), may hold values from -1.5 to 1.5
- exp_avg: float32 [3072, 3072], P('dp', 'seq'), may hold values from -6 to 6
- exp_avg_sq: float32 [3072, 3072], P('dp', 'seq'), may hold values from 0.25 to 4
- left_stats: float32 [3072, 1536], P('dp', 'seq'), as said below
- right_stats: float32 [6144, 3072], P('dp', 'seq')
- left_basis: float32 [3072, 1536], P('dp', 'seq'), may hold values from -0.3125 to 0.3125
- right_basis: float32 [6144, 3072], P('dp', 'seq'), may hold values from -0.21875 to 0.21875
Outputs:
- update: float32 [3072, 3072], P('dp', 'seq')
- new_weight: float32 [3072, 3072], P('dp', 'seq')
- new_exp_avg: float32 [3072, 3072], P('dp', 'seq')
- new_exp_avg_sq: float32 [3072, 3072], P('dp', 'seq')
- new_left_stats: float32 [3072, 1536], P('dp', 'seq')
- new_right_stats: float32 [6144, 3072], P('dp', 'seq')
Inputs may be any that keep to these rules, and one draw needn't show every extreme that they name: Every 384 x 384 block of left_stats and 768 x 768 block of right_stats is symmetric.
All inputs are finite; a program needn't handle non-finite values.
Results may differ from a plain program's by a relative error of at most 0.0003.
Values may be sent and summed in bfloat16 or wider, within the bound.
A program may use at most 128 MiB of HBM per device.

v0:
```python
import jax
import jax.numpy as jnp
from jax import lax
from jax.sharding import PartitionSpec as P

beta_one = 0.9
beta_two = 0.95
epsilon = 1e-08
learn_rate = 0.02
decay_rate = 0.1


def hi_dot(left_mat, right_mat):
    return jnp.dot(left_mat, right_mat, precision=lax.Precision.HIGHEST)


def local(
    attn_out,
    cotangent,
    gate,
    weight,
    exp_avg,
    exp_avg_sq,
    left_stats,
    right_stats,
    left_basis,
    right_basis,
):
    gate_row = gate[0]
    gathered = lax.all_gather(cotangent, "seq", axis=0, tiled=True)
    product = lax.dot_general(
        gathered, attn_out, (((0,), (0,)), ((), ())), preferred_element_type=jnp.float32
    )
    gradient = lax.psum_scatter(gate_row[:, None] * product, "dp", scatter_dimension=0, tiled=True)
    left_new = beta_two * left_stats + (1.0 - beta_two) * hi_dot(gradient, gradient.T)
    right_new = beta_two * right_stats + (1.0 - beta_two) * hi_dot(gradient.T, gradient)
    moment = beta_one * exp_avg + (1.0 - beta_one) * gradient

    def rotate_in(matrix):
        return hi_dot(hi_dot(left_basis.T, matrix), right_basis)

    rotated = rotate_in(gradient)
    second = beta_two * exp_avg_sq + (1.0 - beta_two) * rotated * rotated
    direction = rotate_in(moment) / (jnp.sqrt(second) + epsilon)
    update = hi_dot(hi_dot(left_basis, direction), right_basis.T)
    new_weight = weight * (1.0 - learn_rate * decay_rate) - learn_rate * update
    return (update, new_weight, moment, second, left_new, right_new)


def solution(mesh):
    in_specs = (
        P("dp", "seq"),
        P(("seq", "dp"), None),
        P("dp", None),
        P("dp", "seq"),
        P("dp", "seq"),
        P("dp", "seq"),
        P("dp", "seq"),
        P("dp", "seq"),
        P("dp", "seq"),
        P("dp", "seq"),
    )
    out_specs = (
        P("dp", "seq"),
        P("dp", "seq"),
        P("dp", "seq"),
        P("dp", "seq"),
        P("dp", "seq"),
        P("dp", "seq"),
    )
    return jax.shard_map(local, mesh=mesh, in_specs=in_specs, out_specs=out_specs, check_vma=False)
```

profile of v0, /device:TPU:0, one launch (start us, length us, event | category | flops | bytes accessed | tf_op | source)
XLA Modules:
  0.0 291.6 jit_solution(8672744100477906920)
XLA Ops:
  7.2 0.0 copy-start
  7.2 0.0 copy-start.10
  7.2 0.0 all-gather.2.cloned.1.call-start
  7.2 0.7 all-gather.2.cloned.1.call-update
  7.9 0.0 reduce-scatter.2.cloned.1.call-start
  8.0 127.1 %all-gather.2.cloned.1.call-done = bf16[2048,3072]{1,0:T(8,128)(2,1)} async-done(((bf16[512,3072]{1,0:T(8,128)(2,1)}), bf16[2048,3072]{1,0:T(8,128)(2,1)}) %all-gather.2.cloned.1.call-update) | async-done | bytes 12582928 | tf_op jit(solution)/shard_map/all_gather | solution.py:30
  135.1 0.0 copy-done
  135.1 0.0 copy-done.10
  135.1 15.5 %convolution_multiply_fusion = f32[3072,768]{1,0:T(8,128)} fusion(bf16[2048,3072]{1,0:T(8,128)(2,1)} %all-gather.2.cloned.1.call-done, bf16[2048,768]{1,0:T(8,128)(2,1)S(1)} %copy-done, f32[3072]{0:T(1024)S(1)} %bitcast.19), kind=kOutput, calls=%fused_computation | convolution fusion | flops 9666035712 | bytes 25178112 | tf_op jit(solution)/shard_map/dot_general | solution.py:31
  150.6 0.0 reduce-scatter.2.cloned.1.call-update
  150.6 99.7 %reduce-scatter.2.cloned.1.call-done = f32[384,768]{1,0:T(8,128)} async-done(((f32[3072,768]{1,0:T(8,128)}), f32[384,768]{1,0:T(8,128)}) %reduce-scatter.2.cloned.1.call-update) | async-done | bytes 1179664 | tf_op jit(solution)/shard_map/reduce_scatter | solution.py:34
  250.3 0.0 copy-start.3
  250.3 1.9 multiply_add_fusion.1
  252.2 0.0 copy-done.3
  252.2 0.0 copy-start.4
  252.2 0.0 copy-start.1
  252.2 0.0 copy-start.8
  252.2 2.5 fusion.2
  254.8 0.0 copy-done.4
  254.8 0.0 copy-done.1
  254.8 0.0 copy-start.2
  254.8 2.5 fusion.3
  257.3 0.0 copy-done.8
  257.3 0.0 copy-done.2
  257.3 3.4 %fusion.1 = f32[384,768]{1,0:T(8,128)S(1)} fusion(f32[384,768]{1,0:T(8,128)S(1)} %copy-done.8, f32[768,384]{1,0:T(8,128)S(1)} %fusion.3, f32[768,768]{1,0:T(8,128)S(1)} %copy-done.2), kind=kOutput, calls=%fused_computation.6 | convolution fusion | flops 2719088640 | bytes 5898240 | tf_op jit(solution)/shard_map/dot_general | solution.py:14
  260.7 0.0 copy-start.5
  260.7 3.5 %convolution_divide_fusion = f32[384,768]{1,0:T(8,128)S(1)} fusion(f32[768,384]{1,0:T(8,128)S(1)} %fusion.2, f32[768,768]{1,0:T(8,128)S(1)} %copy-done.2, f32[384,768]{1,0:T(8,128)S(1)} %fusion.1), kind=kOutput, calls=%fused_computation.3 | convolution fusion | flops 2718498816 | bytes 5898240 | tf_op jit(solution)/shard_map/dot_general | solution.py:14
  264.3 0.0 copy-done.5
  264.3 0.0 copy-start.7
  264.3 4.2 %fusion.4 = f32[768,384]{1,0:T(8,128)S(1)} fusion(f32[384,768]{1,0:T(8,128)S(1)} %convolution_divide_fusion, f32[384,384]{1,0:T(8,128)S(1)} %copy-done.3), kind=kOutput, calls=%fused_computation.11 | convolution fusion | flops 1358954496 | bytes 2949120 | tf_op jit(solution)/shard_map/dot_general | solution.py:14
  268.5 0.0 copy-done.7
  268.5 0.0 copy-start.9
  268.5 7.2 %multiply_subtract_fusion = (f32[384,768]{1,0:T(8,128)}, f32[384,768]{1,0:T(8,128)}) fusion(f32[384,768]{1,0:T(8,128)S(1)} %copy-done.7, f32[768,384]{1,0:T(8,128)S(1)} %fusion.4, f32[768,768]{1,0:T(8,128)S(1)} %copy-done.2), kind=kOutput, calls=%fused_computation.7 | convolution fusion | flops 2718793728 | bytes 7077888 | tf_op jit(solution)/shard_map/dot_general | solution.py:14
  275.8 0.0 copy-done.9
  275.8 0.0 copy-start.6
  275.8 2.9 fusion
  278.7 0.0 copy-done.6
  278.7 6.1 %multiply_add_fusion = f32[768,768]{1,0:T(8,128)} fusion(f32[768,768]{1,0:T(8,128)S(1)} %copy-done.6, f32[384,768]{1,0:T(8,128)S(1)} %copy-done.1), kind=kOutput, calls=%fused_computation.1 | convolution fusion | flops 2719678464 | bytes 5898240 | tf_op jit(solution)/shard_map/dot_general | solution.py:14
Async XLA Ops:
  7.2 128.0 %copy-start = (bf16[2048,768]{1,0:T(8,128)(2,1)S(1)}, bf16[2048,768]{1,0:T(8,128)(2,1)}, u32[]{:S(2)}) copy-start(bf16[2048,768]{1,0:T(8,128)(2,1)} %param.10) | copy-start | bytes 9437188
  7.2 127.9 %copy-start.10 = (f32[1,3072]{1,0:T(1,128)S(1)}, f32[1,3072]{1,0:T(1,128)}, u32[]{:S(2)}) copy-start(f32[1,3072]{1,0:T(1,128)} %param.12) | copy-start | bytes 36868
  7.2 127.9 %all-gather.2.cloned.1.call-start = ((), (), s32[]{:S(2)}) async-start(), calls=%async_computation.1 | async-start | bytes 15728640 | tf_op jit(solution)/shard_map/all_gather | solution.py:30
  7.9 242.4 %reduce-scatter.2.cloned.1.call-start = ((), (), s32[]{:S(2)}) async-start(), calls=%async_computation.2 | async-start | bytes 10616832 | tf_op jit(solution)/shard_map/reduce_scatter | solution.py:34
  250.3 1.9 copy-start.3
  252.2 2.6 copy-start.4
  252.2 2.6 copy-start.1
  252.2 5.1 %copy-start.8 = (f32[384,768]{1,0:T(8,128)S(1)}, f32[384,768]{1,0:T(8,128)}, u32[]{:S(2)}) copy-start(f32[384,768]{1,0:T(8,128)} %param.15) | copy-start | bytes 3538948
  254.8 2.5 copy-start.2
  260.7 3.6 %copy-start.5 = (f32[384,768]{1,0:T(8,128)}, f32[384,768]{1,0:T(8,128)S(1)}, u32[]{:S(2)}) copy-start(f32[384,768]{1,0:T(8,128)S(1)} %fusion.1) | copy-start | bytes 3538948
  264.3 4.2 %copy-start.7 = (f32[384,768]{1,0:T(8,128)S(1)}, f32[384,768]{1,0:T(8,128)}, u32[]{:S(2)}) copy-start(f32[384,768]{1,0:T(8,128)} %param.13) | copy-start | bytes 3538948
  268.5 7.3 %copy-start.9 = (f32[384,384]{1,0:T(8,128)S(1)}, f32[384,384]{1,0:T(8,128)}, u32[]{:S(2)}) copy-start(f32[384,384]{1,0:T(8,128)} %param.16) | copy-start | bytes 1769476
  275.8 2.9 copy-start.6
Sparse Core Ops, SparseCore 0:
  9.9 125.2 all-gather.1
  150.7 99.5 reduce-scatter.1
where the time goes:
time: 292 us
  waiting for transfers between devices  228 us (78%)
  matrix products  47.9 us (16%)
  between operations  14.2 us (5%)
    all_gather x1, waiting for transfers between devices, local(): gathered = lax.all_gather(cotangent, 'seq', axis=0, tiled=True)  127 us
    reduce_scatter x1, waiting for transfers between devices, local(): lax.psum_scatter(gate_row[:, None] * product, 'dp', scatter_dimension=0,...  99.7 us
    dot_general x8, matrix products, hi_dot(): return jnp.dot(left_mat, right_mat, precision=lax.Precision.HIGHEST)  32.4 us
    dot_general x1, matrix products, local(): lax.dot_general(gathered, attn_out, (((0,), (0,)), ((), ())), preferred_e...  15.5 us
  transfers between devices with their start and end apart: 2, of which 2 were waited for; matrix products, arithmetic and copies ran while one was open for 0% of the time, Pallas kernels for 0%

commit v1 on v0

v1 whole, which is shorter than its diff:
```python
import functools

import jax
import jax.numpy as jnp
from jax import lax
from jax.experimental import pallas as pl
from jax.experimental.pallas import tpu as pltpu
from jax.sharding import PartitionSpec as P

beta_one = 0.9
beta_two = 0.95
epsilon = 1e-08
learn_rate = 0.02
decay_rate = 0.1

MESH = pl.DeviceIdType.MESH
BLOCKS = 8
AHEAD = 3


def fine_dot(left_mat, right_mat):
    return jnp.dot(left_mat, right_mat, precision=lax.Precision.HIGH)


def gradient_kernel(
    cot_hbm,
    attn_hbm,
    gate_ref,
    grad_ref,
    gath,
    attn,
    acc,
    pair_out,
    pair_in,
    sums,
    relay_in,
    line_in,
    own_sem,
    attn_sem,
    send_x,
    send_y,
    recv_x,
    recv_y,
    pass_x,
    pass_y,
    diag_x,
    diag_y,
    pair_send,
    pair_recv,
    line_send,
    line_recv,
    relay_recv,
):
    tok = cot_hbm.shape[0]
    half = tok // 2
    rows = grad_ref.shape[0]
    s = lax.axis_index("seq")
    d = lax.axis_index("dp")
    x_peer = s + 1 - 2 * (s % 2)
    y_peer = (s + 2) % 4
    diag = 3 - s
    z, core = d // 2, d % 2
    other = z * 2 + 1 - core
    side = z // 2
    far_end = 3 - 3 * side
    far_mid = 2 - side
    near = side * 4 + 1 - z
    is_end = (z % 3) == 0
    is_mid = (z % 3) != 0

    def block_of(k):
        j, h = k // 2, k % 2
        zj = jnp.where(j == 0, far_end, jnp.where(j == 1, far_mid, jnp.where(j == 2, near, z)))
        cj = jnp.where(h == 0, 1 - core, core)
        return zj * 2 + cj

    def cot_block(k):
        return cot_hbm.at[:, pl.ds(pl.multiple_of(block_of(k) * rows, 128), rows)]

    def part(k, owner, start=0, size=tok):
        return gath.at[k, pl.ds(pl.multiple_of(owner * tok + start, half), size), :]

    def own_copy(k):
        return pltpu.make_async_copy(cot_block(k), part(k, s), own_sem.at[k])

    def remote(src, dst, send, recv, where):
        return pltpu.make_async_remote_copy(
            src_ref=src, dst_ref=dst, send_sem=send, recv_sem=recv, device_id=where, device_id_type=MESH
        )

    def to_x(k):
        return remote(cot_block(k), part(k, s), send_x.at[k], recv_x.at[k], {"seq": x_peer})

    def to_y(k):
        return remote(cot_block(k), part(k, s), send_y.at[k], recv_y.at[k], {"seq": y_peer})

    def relay_y(k):
        piece = part(k, x_peer, 0, half)
        return remote(piece, piece, pass_y.at[k], diag_y.at[k], {"seq": y_peer})

    def relay_x(k):
        piece = part(k, y_peer, half, half)
        return remote(piece, piece, pass_x.at[k], diag_x.at[k], {"seq": x_peer})

    def from_x(k):
        return remote(part(k, x_peer), part(k, x_peer), send_x.at[k], recv_x.at[k], {"seq": x_peer})

    def from_y(k):
        return remote(part(k, y_peer), part(k, y_peer), send_y.at[k], recv_y.at[k], {"seq": y_peer})

    def diag_from_y(k):
        piece = part(k, diag, 0, half)
        return remote(piece, piece, pass_y.at[k], diag_y.at[k], {"seq": y_peer})

    def diag_from_x(k):
        piece = part(k, diag, half, half)
        return remote(piece, piece, pass_x.at[k], diag_x.at[k], {"seq": x_peer})

    def to_other(j):
        return remote(pair_out.at[j], pair_in.at[j], pair_send.at[j], pair_recv.at[j], {"dp": other})

    def line(j, dst, recv, z_to):
        return remote(sums.at[j], dst, line_send.at[j], recv, {"dp": z_to * 2 + core})

    attn_copy = pltpu.make_async_copy(attn_hbm, attn, attn_sem)
    attn_copy.start()

    @pl.loop(0, BLOCKS)
    def _(k):
        own_copy(k).start()

    barrier = pltpu.get_barrier_semaphore()
    for where in (
        {"seq": x_peer},
        {"seq": y_peer},
        {"dp": other},
        {"dp": ((z + 1) % 4) * 2 + core},
        {"dp": ((z + 2) % 4) * 2 + core},
        {"dp": ((z + 3) % 4) * 2 + core},
    ):
        pl.semaphore_signal(barrier, inc=1, device_id=where, device_id_type=MESH)
    pl.semaphore_wait(barrier, 6)

    @pl.loop(0, AHEAD)
    def _(k):
        to_x(k).start()
        to_y(k).start()

    attn_copy.wait()

    def work(k):
        own_copy(k).wait()
        diag_from_y(k).wait_recv()
        diag_from_x(k).wait_recv()
        product = lax.dot_general(
            gath[k], attn[...], (((0,), (0,)), ((), ())), preferred_element_type=jnp.float32
        )
        gate_row = gate_ref[:, pl.ds(pl.multiple_of(block_of(k) * rows, 128), rows)]
        gate_col = jnp.transpose(jnp.broadcast_to(gate_row, (128, rows)))[:, :1]
        acc[...] = product * gate_col
        j, h = k // 2, k % 2

        @pl.when(h == 0)
        def _():
            pair_out[j] = acc[...]
            to_other(j).start()

        @pl.when(h == 1)
        def _():
            to_other(j).wait_recv()

            @pl.when(j < 3)
            def _():
                sums[j] = acc[...] + pair_in[j]

            @pl.when(is_end & (j < 2))
            def _():
                line(j, relay_in.at[j], relay_recv.at[j], near).start()

            @pl.when(j == 2)
            def _():
                line(2, line_in.at[0], line_recv.at[0], near).start()

            @pl.when(is_mid & (j == 1))
            def _():
                line(0, relay_in.at[0], relay_recv.at[0], near).wait_recv()
                sums[0] = sums[0] + relay_in[0]
                line(0, line_in.at[1], line_recv.at[1], far_end).start()

            @pl.when(is_mid & (j == 2))
            def _():
                line(1, relay_in.at[1], relay_recv.at[1], near).wait_recv()
                sums[1] = sums[1] + relay_in[1]
                line(1, line_in.at[1], line_recv.at[1], far_mid).start()

            @pl.when(j == 3)
            def _():
                line(2, line_in.at[0], line_recv.at[0], near).wait_recv()
                line(2, line_in.at[1], line_recv.at[1], near).wait_recv()
                grad_ref[...] = (acc[...] + pair_in[3]) + (line_in[0] + line_in[1])

    @pl.loop(0, BLOCKS + 1)
    def _(k):
        @pl.when(k < BLOCKS)
        def _():
            from_x(k).wait_recv()
            relay_y(k).start()
            from_y(k).wait_recv()
            relay_x(k).start()

        @pl.when(k + AHEAD < BLOCKS)
        def _():
            to_x(k + AHEAD).start()
            to_y(k + AHEAD).start()

        @pl.when(k > 0)
        def _():
            work(k - 1)

    @pl.loop(0, BLOCKS)
    def _(k):
        to_x(k).wait_send()
        to_y(k).wait_send()
        relay_x(k).wait_send()
        relay_y(k).wait_send()

    for j in range(4):
        to_other(j).wait_send()
    for j in range(3):
        line(j, line_in.at[0], line_recv.at[0], near).wait_send()


def fused_gradient(attn_out, cotangent, gate):
    tok, features = cotangent.shape
    all_tok, columns = attn_out.shape
    rows = features // BLOCKS
    dma = pltpu.SemaphoreType.DMA
    block = (rows, columns)
    return pl.pallas_call(
        gradient_kernel,
        out_shape=jax.ShapeDtypeStruct(block, jnp.float32),
        in_specs=[
            pl.BlockSpec(memory_space=pl.ANY),
            pl.BlockSpec(memory_space=pl.ANY),
            pl.BlockSpec(memory_space=pltpu.VMEM),
        ],
        out_specs=pl.BlockSpec(memory_space=pltpu.VMEM),
        scratch_shapes=[
            pltpu.VMEM((BLOCKS, all_tok, rows), jnp.bfloat16),
            pltpu.VMEM((all_tok, columns), jnp.bfloat16),
            pltpu.VMEM(block, jnp.float32),
            pltpu.VMEM((4,) + block, jnp.float32),
            pltpu.VMEM((4,) + block, jnp.float32),
            pltpu.VMEM((3,) + block, jnp.float32),
            pltpu.VMEM((2,) + block, jnp.float32),
            pltpu.VMEM((2,) + block, jnp.float32),
            dma((BLOCKS,)),
            dma,
            dma((BLOCKS,)),
            dma((BLOCKS,)),
            dma((BLOCKS,)),
            dma((BLOCKS,)),
            dma((BLOCKS,)),
            dma((BLOCKS,)),
            dma((BLOCKS,)),
            dma((BLOCKS,)),
            dma((4,)),
            dma((4,)),
            dma((3,)),
            dma((2,)),
            dma((2,)),
        ],
        compiler_params=pltpu.CompilerParams(
            collective_id=0, has_side_effects=True, vmem_limit_bytes=48 * 1024 * 1024
        ),
        cost_estimate=pl.CostEstimate(
            flops=2 * all_tok * features * columns, bytes_accessed=8 * tok * features, transcendentals=0
        ),
    )(cotangent, attn_out, gate)


def plain_gradient(attn_out, cotangent, gate):
    gathered = lax.all_gather(cotangent, "seq", axis=0, tiled=True)
    product = lax.dot_general(
        gathered, attn_out, (((0,), (0,)), ((), ())), preferred_element_type=jnp.float32
    )
    return lax.psum_scatter(gate[0][:, None] * product, "dp", scatter_dimension=0, tiled=True)


def local(
    find_gradient,
    attn_out,
    cotangent,
    gate,
    weight,
    exp_avg,
    exp_avg_sq,
    left_stats,
    right_stats,
    left_basis,
    right_basis,
):
    gradient = find_gradient(attn_out, cotangent, gate)
    left_new = beta_two * left_stats + (1.0 - beta_two) * fine_dot(gradient, gradient.T)
    right_new = beta_two * right_stats + (1.0 - beta_two) * fine_dot(gradient.T, gradient)
    moment = beta_one * exp_avg + (1.0 - beta_one) * gradient

    def rotate_in(matrix):
        return fine_dot(fine_dot(left_basis.T, matrix), right_basis)

    rotated = rotate_in(gradient)
    second = beta_two * exp_avg_sq + (1.0 - beta_two) * rotated * rotated
    direction = rotate_in(moment) / (jnp.sqrt(second) + epsilon)
    update = fine_dot(fine_dot(left_basis, direction), right_basis.T)
    new_weight = weight * (1.0 - learn_rate * decay_rate) - learn_rate * update
    return (update, new_weight, moment, second, left_new, right_new)


def solution(mesh):
    spec = P("dp", "seq")
    in_specs = (spec, P(("seq", "dp"), None), P("dp", None)) + (spec,) * 7
    fits = mesh.shape["seq"] == 4 and mesh.shape["dp"] == BLOCKS
    body = functools.partial(local, fused_gradient if fits else plain_gradient)
    return jax.shard_map(body, mesh=mesh, in_specs=in_specs, out_specs=(spec,) * 6, check_vma=False)
```

time: 292 us -> 152 us (0.52)
  waiting for transfers between devices: 228 us -> 0 us
  Pallas kernels: 0 us -> 129 us
  matrix products: 47.9 us -> 19.1 us
  between operations: 14.2 us -> 0.81 us
    pallas_call x0 -> x1, Pallas kernels: none -> 129 us  [fused_gradient(): pl.pallas_call(gradient_kernel, out_shape=jax.ShapeDtypeStruct(block, jnp...]
    all_gather x1 -> x0, waiting for transfers between devices: 127 us -> none  [local(): gathered = lax.all_gather(cotangent, 'seq', axis=0, tiled=True)]
    reduce_scatter x1 -> x0, waiting for transfers between devices: 99.7 us -> none  [local(): lax.psum_scatter(gate_row[:, None] * product, 'dp', scatter_dimension=0,...]
    dot_general x9 -> x8, matrix products: 47.9 us -> 19.1 us  [fine_dot(): return jnp.dot(left_mat, right_mat, precision=lax.Precision.HIGH)]
  transfers between devices with their start and end apart: 2 -> 0, of which waited for: 2 -> 0; matrix products, arithmetic and copies ran while one was open for 0% -> 0% of each run, Pallas kernels for 0% -> 0%
where the time goes in v1:
time: 152 us
  Pallas kernels  129 us (85%)
  matrix products  19.1 us (13%)
  local copies, waits for them, and re-layouts  2.79 us (2%)
    pallas_call x1, Pallas kernels, fused_gradient(): pl.pallas_call(gradient_kernel, out_shape=jax.ShapeDtypeStruct(block, jnp...  129 us
    dot_general x8, matrix products, fine_dot(): return jnp.dot(left_mat, right_mat, precision=lax.Precision.HIGH)  19.1 us

profile of v1, /device:TPU:0, one launch (start us, length us, event | category | flops | bytes accessed | tf_op | source)
XLA Modules:
  0.0 151.6 jit_solution(2978401600481530055)
XLA Ops:
  0.6 0.0 copy-start
  0.6 0.0 copy-start.1
  0.7 2.0 %copy-done.1 = bf16[512,3072]{1,0:T(8,128)(2,1)S(1)} copy-done((bf16[512,3072]{1,0:T(8,128)(2,1)S(1)}, bf16[512,3072]{1,0:T(8,128)(2,1)}, u32[]{:S(2)}) %copy-start.1) | copy-done | bytes 3145752
  2.7 0.0 copy-start.2
  2.7 0.7 copy-done.2
  3.4 0.0 copy-start.3
  3.4 128.7 %shard_map.145 = f32[384,768]{1,0:T(8,128)S(1)} custom-call(bf16[512,3072]{1,0:T(8,128)(2,1)S(1)} %copy-done.1, bf16[2048,768]{1,0:T(8,128)(2,1)} %attn_hbm.1, f32[1,3072]{1,0:T(1,128)S(1)} %copy-done.2), custom_call_target="tpu_custom_call" | custom-call | flops 9663676416 | bytes 12582912 | tf_op jit(solution)/shard_map/pallas_call | solution.py:239
  132.1 0.0 copy-done.3
  132.1 0.0 copy-start.9
  132.1 1.4 fusion.3
  133.5 0.0 copy-done
  133.5 0.0 copy-done.9
  133.6 0.0 copy-start.7
  133.6 1.9 %fusion.1 = f32[384,768]{1,0:T(8,128)S(1)} fusion(f32[384,768]{1,0:T(8,128)S(1)} %copy-done.9, f32[768,384]{1,0:T(8,128)S(1)} %fusion.3, f32[768,768]{1,0:T(8,128)S(1)} %copy-done), kind=kOutput, calls=%fused_computation.5 | convolution fusion | flops 1360134144 | bytes 5898240 | tf_op jit(solution)/shard_map/dot_general | solution.py:22
  135.5 0.0 copy-done.7
  135.5 0.0 copy-start.5
  135.5 0.2 multiply_add_fusion.1
  135.7 0.0 copy-start.4
  135.7 1.4 fusion.2
  137.1 0.0 copy-done.5
  137.1 0.0 copy-done.4
  137.1 2.1 %convolution_divide_fusion = f32[384,768]{1,0:T(8,128)S(1)} fusion(f32[768,384]{1,0:T(8,128)S(1)} %fusion.2, f32[768,768]{1,0:T(8,128)S(1)} %copy-done, f32[384,768]{1,0:T(8,128)S(1)} %fusion.1), kind=kOutput, calls=%fused_computation.2 | convolution fusion | flops 1359544320 | bytes 5898240 | tf_op jit(solution)/shard_map/dot_general | solution.py:22
  139.2 0.0 copy-start.8
  139.2 2.1 %fusion.4 = f32[768,384]{1,0:T(8,128)S(1)} fusion(f32[384,768]{1,0:T(8,128)S(1)} %convolution_divide_fusion, f32[384,384]{1,0:T(8,128)S(1)} %copy-done.3), kind=kOutput, calls=%fused_computation.10 | convolution fusion | flops 679477248 | bytes 2949120 | tf_op jit(solution)/shard_map/dot_general | solution.py:22
  141.3 0.0 copy-done.8
  141.3 0.0 copy-start.6
  141.3 4.5 %multiply_subtract_fusion = (f32[384,768]{1,0:T(8,128)}, f32[384,768]{1,0:T(8,128)}) fusion(f32[384,768]{1,0:T(8,128)S(1)} %copy-done.8, f32[768,384]{1,0:T(8,128)S(1)} %fusion.4, f32[768,768]{1,0:T(8,128)S(1)} %copy-done), kind=kOutput, calls=%fused_computation.6 | convolution fusion | flops 1359839232 | bytes 7077888 | tf_op jit(solution)/shard_map/dot_general | solution.py:22
  145.8 0.0 copy-done.6
  145.8 0.0 copy-start.10
  145.8 3.8 %multiply_add_fusion = f32[768,768]{1,0:T(8,128)} fusion(f32[768,768]{1,0:T(8,128)S(1)} %copy-done.6, f32[384,768]{1,0:T(8,128)S(1)} %shard_map.145), kind=kOutput, calls=%fused_computation | convolution fusion | flops 1360723968 | bytes 5898240 | tf_op jit(solution)/shard_map/dot_general | solution.py:22
  149.6 0.0 copy-done.10
  149.6 2.0 %fusion = f32[384,384]{1,0:T(8,128)} fusion(f32[384,768]{1,0:T(8,128)S(1)} %shard_map.145, f32[384,384]{1,0:T(8,128)S(1)} %copy-done.10), kind=kOutput, calls=%fused_computation.4 | convolution fusion | flops 679919616 | bytes 2359296 | tf_op jit(solution)/shard_map/dot_general | solution.py:22
Async XLA Ops:
  0.6 132.9 %copy-start = (f32[768,768]{1,0:T(8,128)S(1)}, f32[768,768]{1,0:T(8,128)}, u32[]{:S(2)}) copy-start(f32[768,768]{1,0:T(8,128)} %param.19) | copy-start | bytes 7077892
  0.6 2.0 %copy-start.1 = (bf16[512,3072]{1,0:T(8,128)(2,1)S(1)}, bf16[512,3072]{1,0:T(8,128)(2,1)}, u32[]{:S(2)}) copy-start(bf16[512,3072]{1,0:T(8,128)(2,1)} %cot_hbm.1) | copy-start | bytes 9437188
  2.7 0.7 copy-start.2
  3.4 128.7 %copy-start.3 = (f32[384,384]{1,0:T(8,128)S(1)}, f32[384,384]{1,0:T(8,128)}, u32[]{:S(2)}) copy-start(f32[384,384]{1,0:T(8,128)} %param.18) | copy-start | bytes 1769476
  132.1 1.4 copy-start.9
  133.6 1.9 %copy-start.7 = (f32[384,768]{1,0:T(8,128)S(1)}, f32[384,768]{1,0:T(8,128)}, u32[]{:S(2)}) copy-start(f32[384,768]{1,0:T(8,128)} %param.14) | copy-start | bytes 3538948
  135.5 1.6 %copy-start.5 = (f32[384,768]{1,0:T(8,128)}, f32[384,768]{1,0:T(8,128)S(1)}, u32[]{:S(2)}) copy-start(f32[384,768]{1,0:T(8,128)S(1)} %fusion.1) | copy-start | bytes 3538948
  135.7 1.4 copy-start.4
  139.2 2.1 %copy-start.8 = (f32[384,768]{1,0:T(8,128)S(1)}, f32[384,768]{1,0:T(8,128)}, u32[]{:S(2)}) copy-start(f32[384,768]{1,0:T(8,128)} %param.13) | copy-start | bytes 3538948
  141.3 4.5 %copy-start.6 = (f32[768,768]{1,0:T(8,128)S(1)}, f32[768,768]{1,0:T(8,128)}, u32[]{:S(2)}) copy-start(f32[768,768]{1,0:T(8,128)} %param.17) | copy-start | bytes 7077892
  145.8 3.8 %copy-start.10 = (f32[384,384]{1,0:T(8,128)S(1)}, f32[384,384]{1,0:T(8,128)}, u32[]{:S(2)}) copy-start(f32[384,384]{1,0:T(8,128)} %param.16) | copy-start | bytes 1769476

commit v2 on v1

--- a/solution.py
+++ b/solution.py
@@ -15,18 +15,35 @@
 
 MESH = pl.DeviceIdType.MESH
 BLOCKS = 8
-AHEAD = 3
+PIECES = 3
+AHEAD = 4
 
 
 def fine_dot(left_mat, right_mat):
     return jnp.dot(left_mat, right_mat, precision=lax.Precision.HIGH)
+
+
+def halves(value):
+    high = value.astype(jnp.bfloat16)
+    return high, (value - high.astype(jnp.float32)).astype(jnp.bfloat16)
+
+
+def three_pass(left, right, dims):
+    def one(a, b):
+        return lax.dot_general(a, b, (dims, ((), ())), preferred_element_type=jnp.float32)
+
+    return one(left[0], right[0]) + (one(left[0], right[1]) + one(left[1], right[0]))
 
 
 def gradient_kernel(
     cot_hbm,
     attn_hbm,
     gate_ref,
+    mom_hbm,
+    left_hbm,
+    right_hbm,
     grad_ref,
+    turned_ref,
     gath,
     attn,
     acc,
@@ -35,6 +52,10 @@
     sums,
     relay_in,
     line_in,
+    mom,
+    left,
+    right,
+    side_sem,
     own_sem,
     attn_sem,
     send_x,
@@ -74,14 +95,21 @@
         cj = jnp.where(h == 0, 1 - core, core)
         return zj * 2 + cj
 
-    def cot_block(k):
-        return cot_hbm.at[:, pl.ds(pl.multiple_of(block_of(k) * rows, 128), rows)]
+    wide = rows // PIECES
+
+    def cot_piece(k):
+        start = block_of(k // PIECES) * rows + (k % PIECES) * wide
+        return cot_hbm.at[:, pl.ds(pl.multiple_of(start, 128), wide)]
 
     def part(k, owner, start=0, size=tok):
-        return gath.at[k, pl.ds(pl.multiple_of(owner * tok + start, half), size), :]
+        return gath.at[
+            k // PIECES,
+            pl.ds(pl.multiple_of(owner * tok + start, half), size),
+            pl.ds(pl.multiple_of((k % PIECES) * wide, 128), wide),
+        ]
 
     def own_copy(k):
-        return pltpu.make_async_copy(cot_block(k), part(k, s), own_sem.at[k])
+        return pltpu.make_async_copy(cot_piece(k), part(k, s), own_sem.at[k])
 
     def remote(src, dst, send, recv, where):
         return pltpu.make_async_remote_copy(
@@ -89,10 +117,10 @@
         )
 
     def to_x(k):
-        return remote(cot_block(k), part(k, s), send_x.at[k], recv_x.at[k], {"seq": x_peer})
+        return remote(cot_piece(k), part(k, s), send_x.at[k], recv_x.at[k], {"seq": x_peer})
 
     def to_y(k):
-        return remote(cot_block(k), part(k, s), send_y.at[k], recv_y.at[k], {"seq": y_peer})
+        return remote(cot_piece(k), part(k, s), send_y.at[k], recv_y.at[k], {"seq": y_peer})
 
     def relay_y(k):
         piece = part(k, x_peer, 0, half)
@@ -124,8 +152,15 @@
 
     attn_copy = pltpu.make_async_copy(attn_hbm, attn, attn_sem)
     attn_copy.start()
-
-    @pl.loop(0, BLOCKS)
+    side_copies = [
+        pltpu.make_async_copy(src, dst, side_sem.at[n])
+        for n, (src, dst) in enumerate(((mom_hbm, mom), (left_hbm, left), (right_hbm, right)))
+    ]
+    for copy in side_copies:
+        copy.start()
+    steps = BLOCKS * PIECES
+
+    @pl.loop(0, steps)
     def _(k):
         own_copy(k).start()
 
@@ -146,12 +181,17 @@
         to_x(k).start()
         to_y(k).start()
 
+    for copy in side_copies:
+        copy.wait()
+    partial_turn = three_pass(halves(left[...]), halves(mom[...]), ((0,), (0,)))
+    turned_ref[...] = three_pass(halves(partial_turn), halves(right[...]), ((1,), (0,)))
     attn_copy.wait()
 
     def work(k):
-        own_copy(k).wait()
-        diag_from_y(k).wait_recv()
-        diag_from_x(k).wait_recv()
+        for n in range(PIECES):
+            own_copy(k * PIECES + n).wait()
+            diag_from_y(k * PIECES + n).wait_recv()
+            diag_from_x(k * PIECES + n).wait_recv()
         product = lax.dot_general(
             gath[k], attn[...], (((0,), (0,)), ((), ())), preferred_element_type=jnp.float32
         )
@@ -199,25 +239,25 @@
                 line(2, line_in.at[1], line_recv.at[1], near).wait_recv()
                 grad_ref[...] = (acc[...] + pair_in[3]) + (line_in[0] + line_in[1])
 
-    @pl.loop(0, BLOCKS + 1)
+    @pl.loop(0, steps + 1)
     def _(k):
-        @pl.when(k < BLOCKS)
+        @pl.when(k < steps)
         def _():
             from_x(k).wait_recv()
             relay_y(k).start()
             from_y(k).wait_recv()
             relay_x(k).start()
 
-        @pl.when(k + AHEAD < BLOCKS)
+        @pl.when(k + AHEAD < steps)
         def _():
             to_x(k + AHEAD).start()
             to_y(k + AHEAD).start()
 
-        @pl.when(k > 0)
-        def _():
-            work(k - 1)
-
-    @pl.loop(0, BLOCKS)
+        @pl.when((k > 0) & (k % PIECES == 0))
+        def _():
+            work(k // PIECES - 1)
+
+    @pl.loop(0, steps)
     def _(k):
         to_x(k).wait_send()
         to_y(k).wait_send()
@@ -230,7 +270,7 @@
         line(j, line_in.at[0], line_recv.at[0], near).wait_send()
 
 
-def fused_gradient(attn_out, cotangent, gate):
+def fused_gradient(attn_out, cotangent, gate, exp_avg, left_basis, right_basis):
     tok, features = cotangent.shape
     all_tok, columns = attn_out.shape
     rows = features // BLOCKS
@@ -238,13 +278,16 @@
     block = (rows, columns)
     return pl.pallas_call(
         gradient_kernel,
-        out_shape=jax.ShapeDtypeStruct(block, jnp.float32),
+        out_shape=[jax.ShapeDtypeStruct(block, jnp.float32)] * 2,
         in_specs=[
             pl.BlockSpec(memory_space=pl.ANY),
             pl.BlockSpec(memory_space=pl.ANY),
             pl.BlockSpec(memory_space=pltpu.VMEM),
+            pl.BlockSpec(memory_space=pl.ANY),
+            pl.BlockSpec(memory_space=pl.ANY),
+            pl.BlockSpec(memory_space=pl.ANY),
         ],
-        out_specs=pl.BlockSpec(memory_space=pltpu.VMEM),
+        out_specs=[pl.BlockSpec(memory_space=pltpu.VMEM)] * 2,
         scratch_shapes=[
             pltpu.VMEM((BLOCKS, all_tok, rows), jnp.bfloat16),
             pltpu.VMEM((all_tok, columns), jnp.bfloat16),
@@ -254,16 +297,20 @@
             pltpu.VMEM((3,) + block, jnp.float32),
             pltpu.VMEM((2,) + block, jnp.float32),
             pltpu.VMEM((2,) + block, jnp.float32),
-            dma((BLOCKS,)),
+            pltpu.VMEM(block, jnp.float32),
+            pltpu.VMEM((rows, rows), jnp.float32),
+            pltpu.VMEM((columns, columns), jnp.float32),
+            dma((3,)),
+            dma((BLOCKS * PIECES,)),
             dma,
-            dma((BLOCKS,)),
-            dma((BLOCKS,)),
-            dma((BLOCKS,)),
-            dma((BLOCKS,)),
-            dma((BLOCKS,)),
-            dma((BLOCKS,)),
-            dma((BLOCKS,)),
-            dma((BLOCKS,)),
+            dma((BLOCKS * PIECES,)),
+            dma((BLOCKS * PIECES,)),
+            dma((BLOCKS * PIECES,)),
+            dma((BLOCKS * PIECES,)),
+            dma((BLOCKS * PIECES,)),
+            dma((BLOCKS * PIECES,)),
+            dma((BLOCKS * PIECES,)),
+            dma((BLOCKS * PIECES,)),
             dma((4,)),
             dma((4,)),
             dma((3,)),
@@ -271,20 +318,21 @@
             dma((2,)),
         ],
         compiler_params=pltpu.CompilerParams(
-            collective_id=0, has_side_effects=True, vmem_limit_bytes=48 * 1024 * 1024
+            collective_id=0, has_side_effects=True, vmem_limit_bytes=58 * 1024 * 1024
         ),
         cost_estimate=pl.CostEstimate(
             flops=2 * all_tok * features * columns, bytes_accessed=8 * tok * features, transcendentals=0
         ),
-    )(cotangent, attn_out, gate)
-
-
-def plain_gradient(attn_out, cotangent, gate):
+    )(cotangent, attn_out, gate, exp_avg, left_basis, right_basis)
+
+
+def plain_gradient(attn_out, cotangent, gate, exp_avg, left_basis, right_basis):
     gathered = lax.all_gather(cotangent, "seq", axis=0, tiled=True)
     product = lax.dot_general(
         gathered, attn_out, (((0,), (0,)), ((), ())), preferred_element_type=jnp.float32
     )
-    return lax.psum_scatter(gate[0][:, None] * product, "dp", scatter_dimension=0, tiled=True)
+    gradient = lax.psum_scatter(gate[0][:, None] * product, "dp", scatter_dimension=0, tiled=True)
+    return gradient, fine_dot(fine_dot(left_basis.T, exp_avg), right_basis)
 
 
 def local(
@@ -300,17 +348,15 @@
     left_basis,
     right_basis,
 ):
-    gradient = find_gradient(attn_out, cotangent, gate)
+    gradient, turned = find_gradient(
+        attn_out, cotangent, gate, exp_avg, left_basis, right_basis
+    )
     left_new = beta_two * left_stats + (1.0 - beta_two) * fine_dot(gradient, gradient.T)
     right_new = beta_two * right_stats + (1.0 - beta_two) * fine_dot(gradient.T, gradient)
     moment = beta_one * exp_avg + (1.0 - beta_one) * gradient
-
-    def rotate_in(matrix):
-        return fine_dot(fine_dot(left_basis.T, matrix), right_basis)
-
-    rotated = rotate_in(gradient)
+    rotated = fine_dot(fine_dot(left_basis.T, gradient), right_basis)
     second = beta_two * exp_avg_sq + (1.0 - beta_two) * rotated * rotated
-    direction = rotate_in(moment) / (jnp.sqrt(second) + epsilon)
+    direction = (beta_one * turned + (1.0 - beta_one) * rotated) / (jnp.sqrt(second) + epsilon)
     update = fine_dot(fine_dot(left_basis, direction), right_basis.T)
     new_weight = weight * (1.0 - learn_rate * decay_rate) - learn_rate * update
     return (update, new_weight, moment, second, left_new, right_new)

time: 152 us -> 144 us (0.947)
  Pallas kernels: 129 us -> 124 us
  local copies, waits for them, and re-layouts: 2.79 us -> 0.05 us
  matrix products: 19.1 us -> 17.4 us
    pallas_call x1, Pallas kernels: 129 us -> 124 us  [fused_gradient(): pl.pallas_call(gradient_kernel, out_shape=[jax.ShapeDtypeStruct(block, jn...]
    unnamed x22 -> x20, local copies, waits for them, and re-layouts: 2.79 us -> 0.05 us
    dot_general x8 -> x6, matrix products: 19.1 us -> 17.4 us  [fine_dot(): return jnp.dot(left_mat, right_mat, precision=lax.Precision.HIGH)]
where the time goes in v2:
time: 144 us
  Pallas kernels  124 us (86%)
  matrix products  17.4 us (12%)
    pallas_call x1, Pallas kernels, fused_gradient(): pl.pallas_call(gradient_kernel, out_shape=[jax.ShapeDtypeStruct(block, jn...  124 us
    dot_general x6, matrix products, fine_dot(): return jnp.dot(left_mat, right_mat, precision=lax.Precision.HIGH)  17.4 us

profile of v2, /device:TPU:0, one launch (start us, length us, event | category | flops | bytes accessed | tf_op | source)
XLA Modules:
  0.0 143.6 jit_solution(15627673531727798447)
XLA Ops:
  0.6 0.0 copy-start.8
  0.6 0.0 copy-start.3
  0.7 124.2 %shard_map.145 = (f32[384,768]{1,0:T(8,128)}, f32[384,768]{1,0:T(8,128)}) custom-call(bf16[512,3072]{1,0:T(8,128)(2,1)} %cot_hbm.1, bf16[2048,768]{1,0:T(8,128)(2,1)} %attn_hbm.1, f32[1,3072]{1,0:T(1,128)} %gate_ref.1, f32[384,768]{1,0:T(8,128)} %mom_hbm.1, f32[384,384]{1,0:T(8,128)} %left_hbm.1, f32[768,768]{1,0:T(8,128)} %right_hbm.1), custom_call_target="tpu_custom_call" | custom-call | flops 9663676416 | bytes 12582912 | tf_op jit(solution)/shard_map/pallas_call | solution.py:279
  124.8 0.0 copy-done.8
  124.9 0.0 copy-start.1
  124.9 2.8 %fusion.15 = f32[768,384]{1,0:T(8,128)S(1)} fusion(f32[384,768]{1,0:T(8,128)} %get-tuple-element.9, f32[384,384]{1,0:T(8,128)S(1)} %copy-done.8), kind=kOutput, calls=%fused_computation.20 | convolution fusion | flops 679477248 | bytes 2949120 | tf_op jit(solution)/shard_map/dot_general | solution.py:23
  127.7 0.0 copy-done.3
  127.7 0.0 copy-done.1
  127.7 0.0 copy-start.9
  127.7 1.9 %fusion.1 = (f32[384,768]{1,0:T(8,128)S(1)}, f32[384,768]{1,0:T(8,128)S(1)}) fusion(f32[384,768]{1,0:T(8,128)S(1)} %copy-done.3, f32[768,384]{1,0:T(8,128)S(1)} %fusion.15, f32[768,768]{1,0:T(8,128)S(1)} %copy-done.1), kind=kOutput, calls=%fused_computation.4 | convolution fusion | flops 1360134144 | bytes 7077888 | tf_op jit(solution)/shard_map/dot_general | solution.py:23
  129.7 0.0 copy-start.6
  129.7 0.0 copy-done.9
  129.7 0.0 copy-start.4
  129.7 2.4 %fusion.2 = f32[768,384]{1,0:T(8,128)S(1)} fusion(f32[384,384]{1,0:T(8,128)S(1)} %copy-done.8, f32[384,768]{1,0:T(8,128)S(1)} %get-tuple-element.10, f32[384,768]{1,0:T(8,128)S(1)} %get-tuple-element.11, f32[384,768]{1,0:T(8,128)S(1)} %copy-done.9), kind=kOutput, calls=%fused_computation.7 | convolution fusion | flops 680951808 | bytes 5308416 | tf_op jit(solution)/shard_map/dot_general | solution.py:23
  132.1 0.0 copy-done.6
  132.1 0.0 copy-done.4
  132.1 0.0 copy-start
  132.1 0.0 copy-start.2
  132.1 4.5 %multiply_subtract_fusion = (f32[384,768]{1,0:T(8,128)}, f32[384,768]{1,0:T(8,128)}) fusion(f32[384,768]{1,0:T(8,128)S(1)} %copy-done.4, f32[768,384]{1,0:T(8,128)S(1)} %fusion.2, f32[768,768]{1,0:T(8,128)S(1)} %copy-done.1), kind=kOutput, calls=%fused_computation.6 | convolution fusion | flops 1359839232 | bytes 7077888 | tf_op jit(solution)/shard_map/dot_general | solution.py:23
  136.6 0.0 copy-done
  136.6 0.0 copy-done.2
  136.6 0.0 copy-start.5
  136.6 3.8 %multiply_add_fusion = f32[768,768]{1,0:T(8,128)} fusion(f32[768,768]{1,0:T(8,128)S(1)} %copy-done.2, f32[384,768]{1,0:T(8,128)S(1)} %copy-done), kind=kOutput, calls=%fused_computation | convolution fusion | flops 1360723968 | bytes 5898240 | tf_op jit(solution)/shard_map/dot_general | solution.py:23
  140.4 0.0 copy-done.5
  140.4 0.0 copy-start.7
  140.4 1.2 multiply_add_fusion.1
  141.6 0.0 copy-done.7
  141.7 2.0 %fusion = f32[384,384]{1,0:T(8,128)} fusion(f32[384,768]{1,0:T(8,128)S(1)} %copy-done, f32[384,384]{1,0:T(8,128)S(1)} %copy-done.7), kind=kOutput, calls=%fused_computation.3 | convolution fusion | flops 679919616 | bytes 2359296 | tf_op jit(solution)/shard_map/dot_general | solution.py:23
Async XLA Ops:
  0.6 124.2 %copy-start.8 = (f32[384,384]{1,0:T(8,128)S(1)}, f32[384,384]{1,0:T(8,128)}, u32[]{:S(2)}) copy-start(f32[384,384]{1,0:T(8,128)} %left_hbm.1) | copy-start | bytes 1769476
  0.6 127.0 %copy-start.3 = (f32[384,768]{1,0:T(8,128)S(1)}, f32[384,768]{1,0:T(8,128)}, u32[]{:S(2)}) copy-start(f32[384,768]{1,0:T(8,128)} %param.15) | copy-start | bytes 3538948
  124.9 2.8 %copy-start.1 = (f32[768,768]{1,0:T(8,128)S(1)}, f32[768,768]{1,0:T(8,128)}, u32[]{:S(2)}) copy-start(f32[768,768]{1,0:T(8,128)} %right_hbm.1) | copy-start | bytes 7077892
  127.7 2.0 %copy-start.9 = (f32[384,768]{1,0:T(8,128)S(1)}, f32[384,768]{1,0:T(8,128)}, u32[]{:S(2)}) copy-start(f32[384,768]{1,0:T(8,128)} %get-tuple-element.8) | copy-start | bytes 3538948
  129.7 2.4 %copy-start.6 = (f32[384,768]{1,0:T(8,128)}, f32[384,768]{1,0:T(8,128)S(1)}, u32[]{:S(2)}) copy-start(f32[384,768]{1,0:T(8,128)S(1)} %get-tuple-element.10) | copy-start | bytes 3538948
  129.7 2.4 %copy-start.4 = (f32[384,768]{1,0:T(8,128)S(1)}, f32[384,768]{1,0:T(8,128)}, u32[]{:S(2)}) copy-start(f32[384,768]{1,0:T(8,128)} %param.13) | copy-start | bytes 3538948
  132.1 4.5 %copy-start = (f32[384,768]{1,0:T(8,128)S(1)}, f32[384,768]{1,0:T(8,128)}, u32[]{:S(2)}) copy-start(f32[384,768]{1,0:T(8,128)} %get-tuple-element.9) | copy-start | bytes 3538948
  132.1 4.5 %copy-start.2 = (f32[768,768]{1,0:T(8,128)S(1)}, f32[768,768]{1,0:T(8,128)}, u32[]{:S(2)}) copy-start(f32[768,768]{1,0:T(8,128)} %param.17) | copy-start | bytes 7077892
  136.6 3.8 %copy-start.5 = (f32[384,768]{1,0:T(8,128)S(1)}, f32[384,768]{1,0:T(8,128)}, u32[]{:S(2)}) copy-start(f32[384,768]{1,0:T(8,128)} %mom_hbm.1) | copy-start | bytes 3538948
  140.4 1.2 copy-start.7

commit v3 on v2

--- a/solution.py
+++ b/solution.py
@@ -326,6 +326,64 @@
     )(cotangent, attn_out, gate, exp_avg, left_basis, right_basis)
 
 
+def finish_kernel(grad_ref, turned_ref, *refs):
+    sources, targets = refs[:7], refs[7:13]
+    weight, exp_avg, exp_sq, left_old, right_old, left, right = held = refs[13:20]
+    update, weight_new, moment, second, left_new, right_new = made = refs[20:26]
+    in_sem, out_sem = refs[26:]
+    arrive = [pltpu.make_async_copy(sources[n], held[n], in_sem.at[n]) for n in range(7)]
+    leave = [pltpu.make_async_copy(made[n], targets[n], out_sem.at[n]) for n in range(6)]
+    for n in (4, 3, 5, 6, 1, 2, 0):
+        arrive[n].start()
+    grad = grad_ref[...]
+    grad_h = halves(grad)
+    right_gram = three_pass(grad_h, grad_h, ((0,), (0,)))
+    arrive[4].wait()
+    right_new[...] = beta_two * right_old[...] + (1.0 - beta_two) * right_gram
+    leave[5].start()
+    left_gram = three_pass(grad_h, grad_h, ((1,), (1,)))
+    arrive[3].wait()
+    left_new[...] = beta_two * left_old[...] + (1.0 - beta_two) * left_gram
+    leave[4].start()
+    arrive[1].wait()
+    moment[...] = beta_one * exp_avg[...] + (1.0 - beta_one) * grad
+    leave[2].start()
+    arrive[5].wait()
+    left_h = halves(left[...])
+    partial_in = three_pass(left_h, grad_h, ((0,), (0,)))
+    arrive[6].wait()
+    right_h = halves(right[...])
+    rotated = three_pass(halves(partial_in), right_h, ((1,), (0,)))
+    arrive[2].wait()
+    second[...] = beta_two * exp_sq[...] + (1.0 - beta_two) * rotated * rotated
+    leave[3].start()
+    turned = beta_one * turned_ref[...] + (1.0 - beta_one) * rotated
+    direction = turned / (jnp.sqrt(second[...]) + epsilon)
+    partial_back = three_pass(left_h, halves(direction), ((1,), (0,)))
+    update[...] = three_pass(halves(partial_back), right_h, ((1,), (1,)))
+    leave[0].start()
+    arrive[0].wait()
+    weight_new[...] = weight[...] * (1.0 - learn_rate * decay_rate) - learn_rate * update[...]
+    leave[1].start()
+    for copy in leave:
+        copy.wait()
+
+
+def fused_finish(gradient, turned, *arrays):
+    weight, left_stats, right_stats = arrays[0], arrays[3], arrays[4]
+    shapes = [weight.shape] * 4 + [left_stats.shape, right_stats.shape]
+    spaces = [pltpu.VMEM(array.shape, jnp.float32) for array in arrays]
+    spaces += [pltpu.VMEM(shape, jnp.float32) for shape in shapes]
+    return pl.pallas_call(
+        finish_kernel,
+        out_shape=[jax.ShapeDtypeStruct(shape, jnp.float32) for shape in shapes],
+        in_specs=[pl.BlockSpec(memory_space=pltpu.VMEM)] * 2 + [pl.BlockSpec(memory_space=pl.ANY)] * 7,
+        out_specs=[pl.BlockSpec(memory_space=pl.ANY)] * 6,
+        scratch_shapes=spaces + [pltpu.SemaphoreType.DMA((7,)), pltpu.SemaphoreType.DMA((6,))],
+        compiler_params=pltpu.CompilerParams(vmem_limit_bytes=52 * 1024 * 1024),
+    )(gradient, turned, *arrays)
+
+
 def plain_gradient(attn_out, cotangent, gate, exp_avg, left_basis, right_basis):
     gathered = lax.all_gather(cotangent, "seq", axis=0, tiled=True)
     product = lax.dot_general(
@@ -335,11 +393,9 @@
     return gradient, fine_dot(fine_dot(left_basis.T, exp_avg), right_basis)
 
 
-def local(
-    find_gradient,
-    attn_out,
-    cotangent,
-    gate,
+def plain_finish(
+    gradient,
+    turned,
     weight,
     exp_avg,
     exp_avg_sq,
@@ -348,9 +404,6 @@
     left_basis,
     right_basis,
 ):
-    gradient, turned = find_gradient(
-        attn_out, cotangent, gate, exp_avg, left_basis, right_basis
-    )
     left_new = beta_two * left_stats + (1.0 - beta_two) * fine_dot(gradient, gradient.T)
     right_new = beta_two * right_stats + (1.0 - beta_two) * fine_dot(gradient.T, gradient)
     moment = beta_one * exp_avg + (1.0 - beta_one) * gradient
@@ -362,9 +415,17 @@
     return (update, new_weight, moment, second, left_new, right_new)
 
 
+def local(fits, attn_out, cotangent, gate, *arrays):
+    exp_avg, left_basis, right_basis = arrays[1], arrays[5], arrays[6]
+    find = fused_gradient if fits else plain_gradient
+    gradient, turned = find(attn_out, cotangent, gate, exp_avg, left_basis, right_basis)
+    finish = fused_finish if fits else plain_finish
+    return tuple(finish(gradient, turned, *arrays))
+
+
 def solution(mesh):
     spec = P("dp", "seq")
     in_specs = (spec, P(("seq", "dp"), None), P("dp", None)) + (spec,) * 7
     fits = mesh.shape["seq"] == 4 and mesh.shape["dp"] == BLOCKS
-    body = functools.partial(local, fused_gradient if fits else plain_gradient)
+    body = functools.partial(local, fits)
     return jax.shard_map(body, mesh=mesh, in_specs=in_specs, out_specs=(spec,) * 6, check_vma=False)

time: 144 us -> 143 us (level)
  Pallas kernels: 124 us -> 142 us
  matrix products: 17.4 us -> 0 us
    pallas_call x0 -> x1, Pallas kernels: none -> 18 us  [fused_finish(): pl.pallas_call(finish_kernel, out_shape=[jax.ShapeDtypeStruct(shape, jnp....]
    dot_general x6 -> x0, matrix products: 17.4 us -> none  [fine_dot(): return jnp.dot(left_mat, right_mat, precision=lax.Precision.HIGH)]
where the time goes in v3:
time: 143 us
  Pallas kernels  142 us (99%)
    pallas_call x1, Pallas kernels, fused_gradient(): pl.pallas_call(gradient_kernel, out_shape=[jax.ShapeDtypeStruct(block, jn...  124 us
    pallas_call x1, Pallas kernels, fused_finish(): pl.pallas_call(finish_kernel, out_shape=[jax.ShapeDtypeStruct(shape, jnp....  18 us

profile of v3, /device:TPU:0, one launch (start us, length us, event | category | flops | bytes accessed | tf_op | source)
XLA Modules:
  0.0 142.8 jit_solution(14650231918859948299)
XLA Ops:
  0.6 0.0 copy-start
  0.6 0.0 copy-start.1
  0.7 124.0 %shard_map.145 = (f32[384,768]{1,0:T(8,128)}, f32[384,768]{1,0:T(8,128)}) custom-call(bf16[512,3072]{1,0:T(8,128)(2,1)} %cot_hbm.1, bf16[2048,768]{1,0:T(8,128)(2,1)} %attn_hbm.1, f32[1,3072]{1,0:T(1,128)} %gate_ref.1, f32[384,768]{1,0:T(8,128)} %refs_1_.1, f32[384,384]{1,0:T(8,128)} %refs_5_.1, f32[768,768]{1,0:T(8,128)} %refs_6_.1), custom_call_target="tpu_custom_call" | custom-call | flops 9663676416 | bytes 12582912 | tf_op jit(solution)/shard_map/pallas_call | solution.py:279
  124.6 0.0 copy-done
  124.6 0.0 copy-done.1
  124.6 18.0 %shard_map.146 = (f32[384,768]{1,0:T(8,128)}, f32[384,768]{1,0:T(8,128)}, f32[384,768]{1,0:T(8,128)}, f32[384,768]{1,0:T(8,128)}, f32[384,384]{1,0:T(8,128)}, /*index=5*/f32[768,768]{1,0:T(8,128)}) custom-call(f32[384,768]{1,0:T(8,128)} %get-tuple-element.8.grad_ref, f32[384,768]{1,0:T(8,128)} %get-tuple-element.9.turned_ref, f32[384,768]{1,0:T(8,128)} %refs_0_.1, ...), custom_call_target="tpu_custom_call" | custom-call | tf_op jit(solution)/shard_map/pallas_call | solution.py:377
Async XLA Ops:
  0.6 124.0 %copy-start = (f32[384,384]{1,0:T(8,128)S(1)}, f32[384,384]{1,0:T(8,128)}, u32[]{:S(2)}) copy-start(f32[384,384]{1,0:T(8,128)} %refs_5_.1) | copy-start | bytes 1769476
  0.6 124.0 %copy-start.1 = (f32[384,384]{1,0:T(8,128)S(1)}, f32[384,384]{1,0:T(8,128)}, u32[]{:S(2)}) copy-start(f32[384,384]{1,0:T(8,128)} %refs_3_.1) | copy-start | bytes 1769476

commit v4 on v3

--- a/solution.py
+++ b/solution.py
@@ -16,7 +16,7 @@
 MESH = pl.DeviceIdType.MESH
 BLOCKS = 8
 PIECES = 3
-AHEAD = 4
+AHEAD = 7
 
 
 def fine_dot(left_mat, right_mat):

time: 143 us -> 151 us (1.056)
  Pallas kernels: 142 us -> 150 us
    pallas_call x1, Pallas kernels: 124 us -> 132 us  [fused_gradient(): pl.pallas_call(gradient_kernel, out_shape=[jax.ShapeDtypeStruct(block, jn...]
where the time goes in v4:
time: 151 us
  Pallas kernels  150 us (99%)
    pallas_call x1, Pallas kernels, fused_gradient(): pl.pallas_call(gradient_kernel, out_shape=[jax.ShapeDtypeStruct(block, jn...  132 us
    pallas_call x1, Pallas kernels, fused_finish(): pl.pallas_call(finish_kernel, out_shape=[jax.ShapeDtypeStruct(shape, jnp....  18 us

profile of v4, /device:TPU:0, one launch (start us, length us, event | category | flops | bytes accessed | tf_op | source)
XLA Modules:
  0.0 151.2 jit_solution(2694683832429347643)
XLA Ops:
  0.6 0.0 copy-start
  0.6 0.0 copy-start.1
  0.7 132.4 %shard_map.145 = (f32[384,768]{1,0:T(8,128)}, f32[384,768]{1,0:T(8,128)}) custom-call(bf16[512,3072]{1,0:T(8,128)(2,1)} %cot_hbm.1, bf16[2048,768]{1,0:T(8,128)(2,1)} %attn_hbm.1, f32[1,3072]{1,0:T(1,128)} %gate_ref.1, f32[384,768]{1,0:T(8,128)} %refs_1_.1, f32[384,384]{1,0:T(8,128)} %refs_5_.1, f32[768,768]{1,0:T(8,128)} %refs_6_.1), custom_call_target="tpu_custom_call" | custom-call | flops 9663676416 | bytes 12582912 | tf_op jit(solution)/shard_map/pallas_call | solution.py:279
  133.0 0.0 copy-done
  133.1 0.0 copy-done.1
  133.1 18.0 %shard_map.146 = (f32[384,768]{1,0:T(8,128)}, f32[384,768]{1,0:T(8,128)}, f32[384,768]{1,0:T(8,128)}, f32[384,768]{1,0:T(8,128)}, f32[384,384]{1,0:T(8,128)}, /*index=5*/f32[768,768]{1,0:T(8,128)}) custom-call(f32[384,768]{1,0:T(8,128)} %get-tuple-element.8.grad_ref, f32[384,768]{1,0:T(8,128)} %get-tuple-element.9.turned_ref, f32[384,768]{1,0:T(8,128)} %refs_0_.1, ...), custom_call_target="tpu_custom_call" | custom-call | tf_op jit(solution)/shard_map/pallas_call | solution.py:377
Async XLA Ops:
  0.6 132.4 %copy-start = (f32[384,384]{1,0:T(8,128)S(1)}, f32[384,384]{1,0:T(8,128)}, u32[]{:S(2)}) copy-start(f32[384,384]{1,0:T(8,128)} %refs_5_.1) | copy-start | bytes 1769476
  0.6 132.4 %copy-start.1 = (f32[384,384]{1,0:T(8,128)S(1)}, f32[384,384]{1,0:T(8,128)}, u32[]{:S(2)}) copy-start(f32[384,384]{1,0:T(8,128)} %refs_3_.1) | copy-start | bytes 1769476
